TPU v7x, 32 devices: a whole 2x2x4 slice. The times are simulated.
32 devices in a mesh: cases: 2 (over y), tm: 4 (over z), region: 4 (over x, core).
Axes of the slice: x: 2, y: 2, z: 4, core: 2. Of those that a mesh axis runs over, the one named last changes fastest.
Arguments:
- former_estimate: float32 [384, 32, 128], P(('cases', 'tm'), 'region'), parts along dimension 0, may hold values from -6 to 6
- excitation: bfloat16 [384, 32, 128], P(('cases', 'tm'), 'region'), parts along dimension 0, may hold values from -6 to 6
- susceptance_maps: bfloat16 [32, 4, 128, 128], P('region'), may hold values from -0.125 to 0.125
- linked_partner_target: int32 [32, 4], P('region'), may hold values from 0 to 31, as said below
- attenuation: float32 [32, 64], P('region'), may hold values from 0.0002 to 0.03
- revolution_angle: float32 [32, 64], P('region'), may hold values from -0.6 to 0.6
- saturated_flag: int32 [64, 64], P(('cases', 'region')), parts along dimension 0, may hold values 0 or 1
- gain_surge: float32 [384], P(('cases', 'tm')), parts along dimension 0, may hold values from 0.25 to 1
Outputs:
- waveform: float32 [384, 32, 128], P(('cases', 'tm'), 'region'), parts along dimension 0
There are 2 independent parts, one for each index of `cases`. A program takes and returns all parts, laid end to end along the dimension named above; an argument that names none is the same for every part. Nothing has to cross between parts.
Inputs may be any that keep to these rules, and one draw needn't show every extreme that they name: `linked_partner_target`: block row b lies in region g = b // 8. Its column 0 is b itself, column 1 a block of region g, column 2 one of the last 4 blocks of region g - 1 and column 3 one of the first 4 blocks of region g + 1, regions counted around a cycle of 32 // 8.
All inputs are finite; a program needn't handle non-finite values. No bound on the sum of `saturated_flag` on one device may be relied on, other than what follows from the above.
Results may differ from a plain program's by a relative error of at most 0.0017.
Values may be sent and summed in bfloat16 or wider, within the bound.
A program may use at most 64 MiB of HBM per device.

v0:
```python
import jax
import jax.numpy as jnp
from jax import lax
from jax.sharding import PartitionSpec as P

BND = 4
SWEEPS = 3
clip_level = 0.5


def with_halo(block, sides, width):
    for axis, dim in sides:
        count = lax.axis_size(axis)
        forward = [(i, i + 1) for i in range(count - 1)]
        forward.append((count - 1, 0))
        backward = [(target, source) for source, target in forward]
        low = lax.ppermute(
            lax.slice_in_dim(block, block.shape[dim] - width, None, axis=dim), axis, forward
        )
        high = lax.ppermute(lax.slice_in_dim(block, 0, width, axis=dim), axis, backward)
        block = jnp.concatenate([low, block, high], axis=dim)
    return block


def complex_mul(first, second):
    half = first.shape[-1] // 2
    first_re, first_im = (first[..., :half], first[..., half:])
    second_re, second_im = (second[..., :half], second[..., half:])
    return jnp.concatenate(
        [first_re * second_re - first_im * second_im, first_re * second_im + first_im * second_re],
        axis=-1,
    )


def combine(early, late):
    return (complex_mul(late[0], early[0]), complex_mul(late[0], early[1]) + late[1])


def bus_terms(attenuation, revolution_angle):
    modulus = jnp.exp(-attenuation)
    cosine = modulus * jnp.cos(revolution_angle)
    sine = modulus * jnp.sin(revolution_angle)
    argument_spin = jnp.concatenate([cosine, sine], axis=-1)
    input_gain = jnp.sqrt((1.0 - cosine) ** 2 + sine**2)
    return (argument_spin, jnp.concatenate([input_gain, input_gain], axis=-1))


def limit_current(current, saturated_flag):
    half = current.shape[-1] // 2
    square = current[..., :half] ** 2 + current[..., half:] ** 2
    scaling_factor = jnp.where(
        saturated_flag == 1, clip_level / jnp.sqrt(clip_level**2 + square), 1.0
    )
    return current * jnp.concatenate([scaling_factor, scaling_factor], axis=-1)


def periodic_end(total_a, total_b):
    half = total_a.shape[-1] // 2
    denom_re = 1.0 - total_a[..., :half]
    denom_im = -total_a[..., half:]
    square = denom_re**2 + denom_im**2
    conjugate = jnp.concatenate([denom_re / square, -denom_im / square], axis=-1)
    return complex_mul(total_b, conjugate)


def local(
    former_estimate,
    excitation,
    susceptance_maps,
    linked_partner_target,
    attenuation,
    revolution_angle,
    saturated_flag,
    gain_surge,
):
    blocks = former_estimate.shape[1]
    buses = attenuation.shape[1]
    argument_spin, input_gain = bus_terms(attenuation, revolution_angle)
    incremental_spin = gain_surge[:, None, None] * argument_spin[None]
    drive_base = excitation.astype(jnp.float32)
    region_index = lax.axis_index("region")
    network = blocks * lax.axis_size("region")
    local_col = (linked_partner_target - region_index * blocks) % network
    local_col = jnp.where(local_col >= network - BND, local_col - network, local_col) + BND
    unit = jnp.concatenate(
        [jnp.ones((blocks, buses), jnp.float32), jnp.zeros((blocks, buses), jnp.float32)], axis=-1
    )
    nothing = jnp.zeros((blocks, 2 * buses), jnp.float32)
    wave = former_estimate
    for sweep_index in range(SWEEPS):
        rounded = wave.astype(jnp.bfloat16)
        extended = with_halo(rounded, (("region", 1),), BND)
        picked = extended[:, local_col, :]
        current = jnp.einsum(
            "tbkj,bkij->tbi", picked, susceptance_maps, preferred_element_type=jnp.float32
        )
        drive = input_gain[None] * (drive_base - limit_current(current, saturated_flag[None]))
        local_a, local_b = lax.associative_scan(combine, (incremental_spin, drive), axis=0)
        own_map = (local_a[-1], local_b[-1])
        every_a, every_b = (
            lax.all_gather(own_map[0][None], "tm", axis=0, tiled=True),
            lax.all_gather(own_map[1][None], "tm", axis=0, tiled=True),
        )
        run_a, run_b = lax.associative_scan(combine, (every_a, every_b), axis=0)
        total_a, total_b = (run_a[-1], run_b[-1])
        time_index = lax.axis_index("tm")
        earlier = jnp.maximum(time_index - 1, 0)
        prior_a = lax.dynamic_index_in_dim(run_a, earlier, 0, keepdims=False)
        prior_b = lax.dynamic_index_in_dim(run_b, earlier, 0, keepdims=False)
        before = (
            jnp.where(time_index > 0, prior_a, unit),
            jnp.where(time_index > 0, prior_b, nothing),
        )
        end_state = periodic_end(total_a, total_b)
        start_state = complex_mul(before[0], end_state) + before[1]
        wave = complex_mul(local_a, start_state[None]) + local_b
    return wave


def solution(mesh):
    in_specs = (
        P(("cases", "tm"), "region", None),
        P(("cases", "tm"), "region", None),
        P("region", None, None, None),
        P("region", None),
        P("region", None),
        P("region", None),
        P(("cases", "region"), None),
        P(("cases", "tm")),
    )
    out_specs = P(("cases", "tm"), "region", None)
    return jax.shard_map(local, mesh=mesh, in_specs=in_specs, out_specs=out_specs, check_vma=False)
```

profile of v0, /device:TPU:0, one launch (start us, length us, event | category | flops | bytes accessed | tf_op | source)
XLA Modules:
  0.0 90.0 jit_solution(5454847663768018754)
XLA Ops:
  0.0 1.1 %copy.114 = bf16[48,8,128]{2,0,1:T(8,128)(2,1)S(1)} copy(f32[48,8,128]{2,1,0:T(8,128)} %param.8) | data formatting | bytes 294912 | tf_op args[0]
  1.1 0.5 collective-permute-start
  1.6 2.0 %collective-permute-start.1 = (bf16[48,4,128]{2,0,1:T(8,128)(2,1)S(1)}, bf16[48,4,128]{2,0,1:T(8,128)(2,1)S(1)}, u32[]{:S(2)}, u32[]{:S(2)}) collective-permute-start(bf16[48,4,128]{2,0,1:T(8,128)(2,1)S(1)} %get-tuple-element.68), channel_id=1, source_target_pairs={{1,0},{2,1},{3,2},{0,3},{5,4},{6,5},{7,6},{4,7},{9,8},{10,9},{11,1... | collective-permute-start | bytes 147464 | tf_op jit(solution)/shard_map/ppermute | solution.py:20
  3.6 0.7 copy-done.9
  4.5 0.5 copy-done.5
  5.1 0.7 copy-done.10
  5.9 0.6 copy-done.1
  6.6 0.6 gather_fusion
  7.3 0.5 convolution_bitcast_fusion.2
  7.8 0.1 fusion.17
  8.0 0.7 copy-done.2
  8.7 0.1 fusion
  8.9 0.1 multiply_subtract_fusion.5
  12.3 0.1 multiply_subtract_fusion.10
  12.4 0.5 slice-done
  13.0 0.2 pad.790
  13.2 0.2 pad.791
  13.4 14.1 %all_gather.14 = f32[4,8,128]{2,1,0:T(8,128)S(1)} all-gather(f32[1,8,128]{2,1,0:T(8,128)S(1)} %slice_add_fusion.40), channel_id=1, replica_groups=mesh['cases'=2,'tm'=4,'region'=4] {'tm'}, dimensions={0}, use_global_device_ids=true | all-gather | bytes 20480 | tf_op jit(solution)/shard_map/all_gather | solution.py:101
  27.9 0.1 multiply_subtract_fusion.9
  28.1 0.2 pad.226
  28.3 0.2 pad.227
  28.5 13.1 %all_gather.15 = f32[4,8,128]{2,1,0:T(8,128)S(1)} all-gather(f32[1,8,128]{2,1,0:T(8,128)S(1)} %slice_add_fusion.37), channel_id=1, replica_groups=mesh['cases'=2,'tm'=4,'region'=4] {'tm'}, dimensions={0}, use_global_device_ids=true | all-gather | bytes 20480 | tf_op jit(solution)/shard_map/all_gather | solution.py:102
  42.3 0.7 slice-done.1
  43.0 0.7 copy-done.7
  44.0 0.2 multiply_subtract_fusion.2
  44.5 1.7 %collective-permute-start.3 = (bf16[48,4,128]{2,1,0:T(4,128)(2,1)S(1)}, bf16[48,4,128]{2,1,0:T(4,128)(2,1)S(1)}, u32[]{:S(2)}, u32[]{:S(2)}) collective-permute-start(bf16[48,4,128]{2,1,0:T(4,128)(2,1)S(1)} %get-tuple-element.62), channel_id=1, source_target_pairs={{1,0},{2,1},{3,2},{0,3},{5,4},{6,5},{7,6},{4,7},{9,8},{10,9},{11,1... | collective-permute-start | bytes 147464 | tf_op jit(solution)/shard_map/ppermute | solution.py:20
  46.2 1.8 %collective-permute-done.2 = bf16[48,4,128]{2,1,0:T(4,128)(2,1)S(1)} collective-permute-done((bf16[48,4,128]{2,1,0:T(4,128)(2,1)S(1)}, bf16[48,4,128]{2,1,0:T(4,128)(2,1)S(1)}, u32[]{:S(2)}, u32[]{:S(2)}) %collective-permute-start.2) | collective-permute-done | bytes 49184 | tf_op jit(solution)/shard_map/ppermute | solution.py:17
  48.2 0.6 gather_fusion.1
  48.8 0.5 convolution_bitcast_fusion.1
  49.3 0.1 fusion.12
  49.5 0.1 fusion.1
  51.7 0.1 multiply_subtract_fusion.8
  52.0 0.2 pad.240
  52.2 0.2 pad.241
  52.4 13.1 %all_gather.16 = f32[4,8,128]{2,1,0:T(8,128)S(1)} all-gather(f32[1,8,128]{2,1,0:T(8,128)S(1)} %slice_add_fusion.32), channel_id=1, replica_groups=mesh['cases'=2,'tm'=4,'region'=4] {'tm'}, dimensions={0}, use_global_device_ids=true | all-gather | bytes 20480 | tf_op jit(solution)/shard_map/all_gather | solution.py:102
  65.8 0.6 copy-done.4
  67.0 0.1 fusion.19
  67.3 1.7 %collective-permute-start.5 = (bf16[48,4,128]{2,1,0:T(4,128)(2,1)S(1)}, bf16[48,4,128]{2,1,0:T(4,128)(2,1)S(1)}, u32[]{:S(2)}, u32[]{:S(2)}) collective-permute-start(bf16[48,4,128]{2,1,0:T(4,128)(2,1)S(1)} %get-tuple-element.58), channel_id=1, source_target_pairs={{1,0},{2,1},{3,2},{0,3},{5,4},{6,5},{7,6},{4,7},{9,8},{10,9},{11,1... | collective-permute-start | bytes 147464 | tf_op jit(solution)/shard_map/ppermute | solution.py:20
  69.0 1.8 %collective-permute-done.4 = bf16[48,4,128]{2,1,0:T(4,128)(2,1)S(1)} collective-permute-done((bf16[48,4,128]{2,1,0:T(4,128)(2,1)S(1)}, bf16[48,4,128]{2,1,0:T(4,128)(2,1)S(1)}, u32[]{:S(2)}, u32[]{:S(2)}) %collective-permute-start.4) | collective-permute-done | bytes 49184 | tf_op jit(solution)/shard_map/ppermute | solution.py:17
  70.9 0.6 gather_fusion.2
  71.6 0.4 convolution_bitcast_fusion
  72.1 0.1 fusion.7
  72.2 0.1 fusion.2
  74.5 0.1 multiply_subtract_fusion.7
  74.8 0.2 pad.254
  75.0 0.2 pad.255
  75.2 13.1 %all_gather.17 = f32[4,8,128]{2,1,0:T(8,128)S(1)} all-gather(f32[1,8,128]{2,1,0:T(8,128)S(1)} %slice_add_fusion.27), channel_id=1, replica_groups=mesh['cases'=2,'tm'=4,'region'=4] {'tm'}, dimensions={0}, use_global_device_ids=true | all-gather | bytes 20480 | tf_op jit(solution)/shard_map/all_gather | solution.py:102
  89.2 0.8 maximum_add_fusion.2
  (266 shorter events, 11.6 us)
Async XLA Ops:
  0.0 7.3 %copy-start = (bf16[8,4,128,128]{3,2,1,0:T(8,128)(2,1)S(1)}, bf16[8,4,128,128]{3,2,1,0:T(8,128)(2,1)}, u32[]{:S(2)}) copy-start(bf16[8,4,128,128]{3,2,1,0:T(8,128)(2,1)} %param.10) | copy-start | bytes 3145732
  1.1 2.5 %copy-start.8 = (s32[8,64]{1,0:T(8,128)S(1)}, s32[8,64]{1,0:T(8,128)}, u32[]{:S(2)}) copy-start(s32[8,64]{1,0:T(8,128)} %param.14) | copy-start | bytes 6148
  1.1 5.5 %collective-permute-start = (bf16[48,4,128]{2,0,1:T(8,128)(2,1)S(1)}, bf16[48,4,128]{2,0,1:T(8,128)(2,1)S(1)}, u32[]{:S(2)}, u32[]{:S(2)}) collective-permute-start(bf16[48,4,128]{2,0,1:T(8,128)(2,1)S(1)} %get-tuple-element.67), channel_id=1, source_target_pairs={{0,1},{1,2},{2,3},{3,0},{4,5},{5,6},{6,7},{7,4},{8,9},{9,10},{10,1... | collective-permute-start | bytes 147464 | tf_op jit(solution)/shard_map/ppermute | solution.py:17
  1.6 5.0 %collective-permute-start.1 = (bf16[48,4,128]{2,0,1:T(8,128)(2,1)S(1)}, bf16[48,4,128]{2,0,1:T(8,128)(2,1)S(1)}, u32[]{:S(2)}, u32[]{:S(2)}) collective-permute-start(bf16[48,4,128]{2,0,1:T(8,128)(2,1)S(1)} %get-tuple-element.68), channel_id=1, source_target_pairs={{1,0},{2,1},{3,2},{0,3},{5,4},{6,5},{7,6},{4,7},{9,8},{10,9},{11,1... | collective-permute-start | bytes 147464 | tf_op jit(solution)/shard_map/ppermute | solution.py:20
  3.6 0.7 copy-start.9
  4.3 0.7 copy-start.5
  4.3 0.7 copy-start.6
  5.1 0.7 copy-start.10
  5.9 0.7 copy-start.1
  7.8 0.9 copy-start.2
  12.2 0.7 slice-start
  27.5 14.5 %copy-start.3 = (f32[4,8,128]{2,1,0:T(8,128)}, f32[4,8,128]{2,1,0:T(8,128)S(1)}, u32[]{:S(2)}) copy-start(f32[4,8,128]{2,1,0:T(8,128)S(1)} %all_gather.14) | copy-start | bytes 49156
  42.3 0.7 slice-start.1
  43.0 0.7 copy-start.7
  44.4 3.6 %collective-permute-start.2 = (bf16[48,4,128]{2,1,0:T(4,128)(2,1)S(1)}, bf16[48,4,128]{2,1,0:T(4,128)(2,1)S(1)}, u32[]{:S(2)}, u32[]{:S(2)}) collective-permute-start(bf16[48,4,128]{2,1,0:T(4,128)(2,1)S(1)} %get-tuple-element.61), channel_id=1, source_target_pairs={{0,1},{1,2},{2,3},{3,0},{4,5},{5,6},{6,7},{7,4},{8,9},{9,10},{10,1... | collective-permute-start | bytes 147464 | tf_op jit(solution)/shard_map/ppermute | solution.py:17
  44.5 3.5 %collective-permute-start.3 = (bf16[48,4,128]{2,1,0:T(4,128)(2,1)S(1)}, bf16[48,4,128]{2,1,0:T(4,128)(2,1)S(1)}, u32[]{:S(2)}, u32[]{:S(2)}) collective-permute-start(bf16[48,4,128]{2,1,0:T(4,128)(2,1)S(1)} %get-tuple-element.62), channel_id=1, source_target_pairs={{1,0},{2,1},{3,2},{0,3},{5,4},{6,5},{7,6},{4,7},{9,8},{10,9},{11,1... | collective-permute-start | bytes 147464 | tf_op jit(solution)/shard_map/ppermute | solution.py:20
  65.7 0.7 copy-start.4
  67.2 3.6 %collective-permute-start.4 = (bf16[48,4,128]{2,1,0:T(4,128)(2,1)S(1)}, bf16[48,4,128]{2,1,0:T(4,128)(2,1)S(1)}, u32[]{:S(2)}, u32[]{:S(2)}) collective-permute-start(bf16[48,4,128]{2,1,0:T(4,128)(2,1)S(1)} %get-tuple-element.57), channel_id=1, source_target_pairs={{0,1},{1,2},{2,3},{3,0},{4,5},{5,6},{6,7},{7,4},{8,9},{9,10},{10,1... | collective-permute-start | bytes 147464 | tf_op jit(solution)/shard_map/ppermute | solution.py:17
  67.3 3.5 %collective-permute-start.5 = (bf16[48,4,128]{2,1,0:T(4,128)(2,1)S(1)}, bf16[48,4,128]{2,1,0:T(4,128)(2,1)S(1)}, u32[]{:S(2)}, u32[]{:S(2)}) collective-permute-start(bf16[48,4,128]{2,1,0:T(4,128)(2,1)S(1)} %get-tuple-element.58), channel_id=1, source_target_pairs={{1,0},{2,1},{3,2},{0,3},{5,4},{6,5},{7,6},{4,7},{9,8},{10,9},{11,1... | collective-permute-start | bytes 147464 | tf_op jit(solution)/shard_map/ppermute | solution.py:20
where the time goes:
time: 90.4 us; the launch traced here: 90 us
  blocking collectives  53.5 us (59%)
  local copies, waits for them, and re-layouts  12.5 us (14%)
  other arithmetic  11.7 us (13%)
  starting transfers between devices  6.07 us (7%)
  waiting for transfers between devices  3.55 us (4%)
  matrix products  1.36 us (2%)
  between operations  1.28 us (1%)
    all_gather x3, blocking collectives, local(): lax.all_gather(own_map[1][None], 'tm', axis=0, tiled=True)  39.4 us
    all_gather x1, blocking collectives, local(): lax.all_gather(own_map[0][None], 'tm', axis=0, tiled=True)  14.1 us
    unnamed x26, local copies, waits for them, and re-layouts  5.99 us
    ppermute x3, starting transfers between devices, with_halo(): lax.ppermute(lax.slice_in_dim(block, 0, width, axis=dim), axis, backward)  5.45 us
    sub x45, other arithmetic, complex_mul(): first_re * second_re - first_im * second_im  4.13 us
    ppermute x3, waiting for transfers between devices, with_halo(): lax.ppermute(lax.slice_in_dim(block, block.shape[dim] - width, None, axis...  3.54 us
    add x33, other arithmetic, combine(): complex_mul(late[0], early[1]) + late[1]  2.7 us
    pad x34, local copies, waits for them, and re-layouts, local(): lax.associative_scan(combine, (incremental_spin, drive), axis=0)  2.34 us
  transfers between devices with their start and end apart: 6, of which 2 were waited for; matrix products, arithmetic and copies ran while one was open for 0% of the time, Pallas kernels for 0%

commit v1 on v0

--- a/solution.py
+++ b/solution.py
@@ -6,6 +6,24 @@
 BND = 4
 SWEEPS = 3
 clip_level = 0.5
+
+
+def gather_around(shard, axis, dim):
+    ways, here, turn = (lax.axis_size(axis), lax.axis_index(axis), shard.shape[dim])
+    lengths = [n * ways if d == dim else n for d, n in enumerate(shard.shape)]
+    full = lax.dynamic_update_slice_in_dim(
+        jnp.zeros(lengths, shard.dtype), shard, here * turn, axis=dim
+    )
+    going_up = going_down = shard
+    for far in range(1, ways // 2 + 1):
+        going_up = lax.ppermute(going_up, axis, [(d, (d + 1) % ways) for d in range(ways)])
+        full = lax.dynamic_update_slice_in_dim(full, going_up, (here - far) % ways * turn, axis=dim)
+        if 2 * far < ways:
+            going_down = lax.ppermute(going_down, axis, [(d, (d - 1) % ways) for d in range(ways)])
+            full = lax.dynamic_update_slice_in_dim(
+                full, going_down, (here + far) % ways * turn, axis=dim
+            )
+    return full
 
 
 def with_halo(block, sides, width):
@@ -98,7 +116,7 @@
         local_a, local_b = lax.associative_scan(combine, (incremental_spin, drive), axis=0)
         own_map = (local_a[-1], local_b[-1])
         every_a, every_b = (
-            lax.all_gather(own_map[0][None], "tm", axis=0, tiled=True),
+            gather_around(own_map[0][None], "tm", 0),
             lax.all_gather(own_map[1][None], "tm", axis=0, tiled=True),
         )
         run_a, run_b = lax.associative_scan(combine, (every_a, every_b), axis=0)

time: 90.4 us -> 84.8 us (0.938)
  blocking collectives: 53.5 us -> 39.4 us
  waiting for transfers between devices: 3.55 us -> 8.78 us
  starting transfers between devices: 6.07 us -> 10.7 us
  local copies, waits for them, and re-layouts: 12.5 us -> 11.1 us
    all_gather x1 -> x0, blocking collectives: 14.1 us -> none  [local(): lax.all_gather(own_map[0][None], 'tm', axis=0, tiled=True)]
    ppermute x0 -> x3, waiting for transfers between devices: none -> 5.23 us  [the longest x2 5.23 us: gather_around(): lax.ppermute(going_up, axis, [(d, (d + 1) % ways) for d in range(ways)])]
    ppermute x0 -> x3, starting transfers between devices: none -> 4.64 us  [the longest x2 2.55 us: gather_around(): lax.ppermute(going_up, axis, [(d, (d + 1) % ways) for d in range(ways)])]
    unnamed x26 -> x22, local copies, waits for them, and re-layouts: 5.99 us -> 5.28 us
  transfers between devices with their start and end apart: 6 -> 9, of which waited for: 2 -> 3; matrix products, arithmetic and copies ran while one was open for 0% -> 2% of each run, Pallas kernels for 0% -> 0%
where the time goes in v1:
time: 84.8 us; the launch traced here: 84.4 us
  blocking collectives  39.4 us (46%)
  other arithmetic  11.8 us (14%)
  local copies, waits for them, and re-layouts  11.1 us (13%)
  starting transfers between devices  10.7 us (13%)
  waiting for transfers between devices  8.78 us (10%)
  matrix products  1.36 us (2%)
  between operations  1.35 us (2%)
    all_gather x3, blocking collectives, local(): lax.all_gather(own_map[1][None], 'tm', axis=0, tiled=True)  39.4 us
    ppermute x3, starting transfers between devices, with_halo(): lax.ppermute(lax.slice_in_dim(block, 0, width, axis=dim), axis, backward)  5.45 us
    unnamed x22, local copies, waits for them, and re-layouts  5.28 us
    ppermute x2, waiting for transfers between devices, gather_around(): lax.ppermute(going_up, axis, [(d, (d + 1) % ways) for d in range(ways)])  5.23 us
    sub x45, other arithmetic, complex_mul(): first_re * second_re - first_im * second_im  4.14 us
    ppermute x3, waiting for transfers between devices, with_halo(): lax.ppermute(lax.slice_in_dim(block, block.shape[dim] - width, None, axis...  3.54 us
    add x33, other arithmetic, combine(): complex_mul(late[0], early[1]) + late[1]  2.7 us
    ppermute x2, starting transfers between devices, gather_around(): lax.ppermute(going_up, axis, [(d, (d + 1) % ways) for d in range(ways)])  2.55 us
  transfers between devices with their start and end apart: 9, of which 3 were waited for; matrix products, arithmetic and copies ran while one was open for 2% of the time, Pallas kernels for 0%

profile of v1, /device:TPU:0, one launch (start us, length us, event | category | flops | bytes accessed | tf_op | source)
XLA Modules:
  0.0 84.4 jit_solution(15359029266268801044)
XLA Ops:
  0.0 1.1 %copy.117 = bf16[48,8,128]{2,0,1:T(8,128)(2,1)S(1)} copy(f32[48,8,128]{2,1,0:T(8,128)} %param.8) | data formatting | bytes 294912 | tf_op args[0]
  1.1 0.5 collective-permute-start.3
  1.6 2.0 %collective-permute-start.4 = (bf16[48,4,128]{2,0,1:T(8,128)(2,1)S(1)}, bf16[48,4,128]{2,0,1:T(8,128)(2,1)S(1)}, u32[]{:S(2)}, u32[]{:S(2)}) collective-permute-start(bf16[48,4,128]{2,0,1:T(8,128)(2,1)S(1)} %get-tuple-element.70), channel_id=1, source_target_pairs={{1,0},{2,1},{3,2},{0,3},{5,4},{6,5},{7,6},{4,7},{9,8},{10,9},{11,1... | collective-permute-start | bytes 147464 | tf_op jit(solution)/shard_map/ppermute | solution.py:38
  3.6 0.7 copy-done.7
  4.5 0.5 copy-done.3
  5.1 0.7 copy-done.8
  6.0 0.6 copy-done.1
  6.6 0.6 gather_fusion
  7.3 0.5 convolution_bitcast_fusion.2
  7.8 0.1 fusion.17
  8.0 0.7 copy-done.2
  8.7 0.1 fusion
  8.9 0.1 multiply_subtract_fusion.5
  12.3 0.1 multiply_subtract_fusion.10
  12.4 0.5 slice-done
  13.0 0.2 pad.790
  13.2 0.2 pad.791
  13.4 2.4 %collective-permute-start = (f32[1,8,128]{2,1,0:T(8,128)S(1)}, f32[1,8,128]{2,1,0:T(8,128)S(1)}, u32[]{:S(2)}, u32[]{:S(2)}) collective-permute-start(f32[1,8,128]{2,1,0:T(8,128)S(1)} %get-tuple-element.20), channel_id=1, source_target_pairs={{0,4},{4,8},{8,12},{12,0},{1,5},{5,9},{9,13},{13,1},{2,6},{6,10},{... | collective-permute-start | bytes 12296 | tf_op jit(solution)/shard_map/ppermute | solution.py:19
  15.8 2.1 %collective-permute-start.1 = (f32[1,8,128]{2,1,0:T(8,128)S(1)}, f32[1,8,128]{2,1,0:T(8,128)S(1)}, u32[]{:S(2)}, u32[]{:S(2)}) collective-permute-start(f32[1,8,128]{2,1,0:T(8,128)S(1)} %get-tuple-element.20), channel_id=1, source_target_pairs={{0,12},{4,0},{8,4},{12,8},{1,13},{5,1},{9,5},{13,9},{2,14},{6,2},{... | collective-permute-start | bytes 12296 | tf_op jit(solution)/shard_map/ppermute | solution.py:22
  18.2 0.1 multiply_subtract_fusion.9
  18.5 0.2 pad.226
  18.7 0.2 pad.227
  18.9 13.1 %all_gather.9 = f32[4,8,128]{2,1,0:T(8,128)S(1)} all-gather(f32[1,8,128]{2,1,0:T(8,128)S(1)} %slice_add_fusion.37), channel_id=1, replica_groups=mesh['cases'=2,'tm'=4,'region'=4] {'tm'}, dimensions={0}, use_global_device_ids=true | all-gather | bytes 20480 | tf_op jit(solution)/shard_map/all_gather | solution.py:120
  32.0 0.2 collective-permute-start.2
  32.2 5.2 %collective-permute-done.2 = f32[1,8,128]{2,1,0:T(8,128)S(1)} collective-permute-done((f32[1,8,128]{2,1,0:T(8,128)S(1)}, f32[1,8,128]{2,1,0:T(8,128)S(1)}, u32[]{:S(2)}, u32[]{:S(2)}) %collective-permute-start.2) | collective-permute-done | bytes 4128 | tf_op jit(solution)/shard_map/ppermute | solution.py:19
  38.2 0.7 copy-done.5
  39.1 0.2 multiply_subtract_fusion.2
  39.6 1.7 %collective-permute-start.6 = (bf16[48,4,128]{2,1,0:T(4,128)(2,1)S(1)}, bf16[48,4,128]{2,1,0:T(4,128)(2,1)S(1)}, u32[]{:S(2)}, u32[]{:S(2)}) collective-permute-start(bf16[48,4,128]{2,1,0:T(4,128)(2,1)S(1)} %get-tuple-element.64), channel_id=1, source_target_pairs={{1,0},{2,1},{3,2},{0,3},{5,4},{6,5},{7,6},{4,7},{9,8},{10,9},{11,1... | collective-permute-start | bytes 147464 | tf_op jit(solution)/shard_map/ppermute | solution.py:38
  41.3 1.8 %collective-permute-done.5 = bf16[48,4,128]{2,1,0:T(4,128)(2,1)S(1)} collective-permute-done((bf16[48,4,128]{2,1,0:T(4,128)(2,1)S(1)}, bf16[48,4,128]{2,1,0:T(4,128)(2,1)S(1)}, u32[]{:S(2)}, u32[]{:S(2)}) %collective-permute-start.5) | collective-permute-done | bytes 49184 | tf_op jit(solution)/shard_map/ppermute | solution.py:35
  43.3 0.6 gather_fusion.1
  43.9 0.4 convolution_bitcast_fusion.1
  44.4 0.1 fusion.12
  44.6 0.1 fusion.1
  46.8 0.1 multiply_subtract_fusion.8
  47.1 0.2 pad.240
  47.3 0.2 pad.241
  47.5 13.1 %all_gather.10 = f32[4,8,128]{2,1,0:T(8,128)S(1)} all-gather(f32[1,8,128]{2,1,0:T(8,128)S(1)} %slice_add_fusion.32), channel_id=1, replica_groups=mesh['cases'=2,'tm'=4,'region'=4] {'tm'}, dimensions={0}, use_global_device_ids=true | all-gather | bytes 20480 | tf_op jit(solution)/shard_map/all_gather | solution.py:120
  61.7 1.7 %collective-permute-start.8 = (bf16[48,4,128]{2,1,0:T(4,128)(2,1)S(1)}, bf16[48,4,128]{2,1,0:T(4,128)(2,1)S(1)}, u32[]{:S(2)}, u32[]{:S(2)}) collective-permute-start(bf16[48,4,128]{2,1,0:T(4,128)(2,1)S(1)} %get-tuple-element.60), channel_id=1, source_target_pairs={{1,0},{2,1},{3,2},{0,3},{5,4},{6,5},{7,6},{4,7},{9,8},{10,9},{11,1... | collective-permute-start | bytes 147464 | tf_op jit(solution)/shard_map/ppermute | solution.py:38
  63.5 1.8 %collective-permute-done.7 = bf16[48,4,128]{2,1,0:T(4,128)(2,1)S(1)} collective-permute-done((bf16[48,4,128]{2,1,0:T(4,128)(2,1)S(1)}, bf16[48,4,128]{2,1,0:T(4,128)(2,1)S(1)}, u32[]{:S(2)}, u32[]{:S(2)}) %collective-permute-start.7) | collective-permute-done | bytes 49184 | tf_op jit(solution)/shard_map/ppermute | solution.py:35
  65.4 0.6 gather_fusion.2
  66.0 0.5 convolution_bitcast_fusion
  66.6 0.1 fusion.7
  66.7 0.1 fusion.2
  69.0 0.1 multiply_subtract_fusion.7
  69.3 0.2 pad.254
  69.4 0.2 pad.255
  69.6 13.1 %all_gather.11 = f32[4,8,128]{2,1,0:T(8,128)S(1)} all-gather(f32[1,8,128]{2,1,0:T(8,128)S(1)} %slice_add_fusion.27), channel_id=1, replica_groups=mesh['cases'=2,'tm'=4,'region'=4] {'tm'}, dimensions={0}, use_global_device_ids=true | all-gather | bytes 20480 | tf_op jit(solution)/shard_map/all_gather | solution.py:120
  83.6 0.8 maximum_add_fusion.2
  (270 shorter events, 11.8 us)
Async XLA Ops:
  0.0 7.3 %copy-start = (bf16[8,4,128,128]{3,2,1,0:T(8,128)(2,1)S(1)}, bf16[8,4,128,128]{3,2,1,0:T(8,128)(2,1)}, u32[]{:S(2)}) copy-start(bf16[8,4,128,128]{3,2,1,0:T(8,128)(2,1)} %param.10) | copy-start | bytes 3145732
  1.1 2.5 %copy-start.6 = (s32[8,64]{1,0:T(8,128)S(1)}, s32[8,64]{1,0:T(8,128)}, u32[]{:S(2)}) copy-start(s32[8,64]{1,0:T(8,128)} %param.14) | copy-start | bytes 6148
  1.1 5.5 %collective-permute-start.3 = (bf16[48,4,128]{2,0,1:T(8,128)(2,1)S(1)}, bf16[48,4,128]{2,0,1:T(8,128)(2,1)S(1)}, u32[]{:S(2)}, u32[]{:S(2)}) collective-permute-start(bf16[48,4,128]{2,0,1:T(8,128)(2,1)S(1)} %get-tuple-element.69), channel_id=1, source_target_pairs={{0,1},{1,2},{2,3},{3,0},{4,5},{5,6},{6,7},{7,4},{8,9},{9,10},{10,1... | collective-permute-start | bytes 147464 | tf_op jit(solution)/shard_map/ppermute | solution.py:35
  1.6 5.0 %collective-permute-start.4 = (bf16[48,4,128]{2,0,1:T(8,128)(2,1)S(1)}, bf16[48,4,128]{2,0,1:T(8,128)(2,1)S(1)}, u32[]{:S(2)}, u32[]{:S(2)}) collective-permute-start(bf16[48,4,128]{2,0,1:T(8,128)(2,1)S(1)} %get-tuple-element.70), channel_id=1, source_target_pairs={{1,0},{2,1},{3,2},{0,3},{5,4},{6,5},{7,6},{4,7},{9,8},{10,9},{11,1... | collective-permute-start | bytes 147464 | tf_op jit(solution)/shard_map/ppermute | solution.py:38
  3.6 0.7 copy-start.7
  4.3 0.7 copy-start.3
  4.3 0.7 copy-start.4
  5.1 0.7 copy-start.8
  5.9 0.7 copy-start.1
  7.8 0.9 %copy-start.2 = (bf16[48,8,128]{2,1,0:T(8,128)(2,1)S(1)}, bf16[48,8,128]{2,1,0:T(8,128)(2,1)}, u32[]{:S(2)}) copy-start(bf16[48,8,128]{2,1,0:T(8,128)(2,1)} %param.9) | copy-start | bytes 294916
  12.2 0.7 slice-start
  13.4 18.6 %collective-permute-start = (f32[1,8,128]{2,1,0:T(8,128)S(1)}, f32[1,8,128]{2,1,0:T(8,128)S(1)}, u32[]{:S(2)}, u32[]{:S(2)}) collective-permute-start(f32[1,8,128]{2,1,0:T(8,128)S(1)} %get-tuple-element.20), channel_id=1, source_target_pairs={{0,4},{4,8},{8,12},{12,0},{1,5},{5,9},{9,13},{13,1},{2,6},{6,10},{... | collective-permute-start | bytes 12296 | tf_op jit(solution)/shard_map/ppermute | solution.py:19
  15.8 16.4 %collective-permute-start.1 = (f32[1,8,128]{2,1,0:T(8,128)S(1)}, f32[1,8,128]{2,1,0:T(8,128)S(1)}, u32[]{:S(2)}, u32[]{:S(2)}) collective-permute-start(f32[1,8,128]{2,1,0:T(8,128)S(1)} %get-tuple-element.20), channel_id=1, source_target_pairs={{0,12},{4,0},{8,4},{12,8},{1,13},{5,1},{9,5},{13,9},{2,14},{6,2},{... | collective-permute-start | bytes 12296 | tf_op jit(solution)/shard_map/ppermute | solution.py:22
  32.0 5.4 %collective-permute-start.2 = (f32[1,8,128]{2,1,0:T(8,128)S(1)}, f32[1,8,128]{2,1,0:T(8,128)S(1)}, u32[]{:S(2)}, u32[]{:S(2)}) collective-permute-start(f32[1,8,128]{2,1,0:T(8,128)S(1)} %collective-permute-done), channel_id=1, source_target_pairs={{0,4},{4,8},{8,12},{12,0},{1,5},{5,9},{9,13},{13,1},{2,6},{6,10},{... | collective-permute-start | bytes 12296 | tf_op jit(solution)/shard_map/ppermute | solution.py:19
  38.1 0.7 copy-start.5
  39.5 3.6 %collective-permute-start.5 = (bf16[48,4,128]{2,1,0:T(4,128)(2,1)S(1)}, bf16[48,4,128]{2,1,0:T(4,128)(2,1)S(1)}, u32[]{:S(2)}, u32[]{:S(2)}) collective-permute-start(bf16[48,4,128]{2,1,0:T(4,128)(2,1)S(1)} %get-tuple-element.63), channel_id=1, source_target_pairs={{0,1},{1,2},{2,3},{3,0},{4,5},{5,6},{6,7},{7,4},{8,9},{9,10},{10,1... | collective-permute-start | bytes 147464 | tf_op jit(solution)/shard_map/ppermute | solution.py:35
  39.6 3.5 %collective-permute-start.6 = (bf16[48,4,128]{2,1,0:T(4,128)(2,1)S(1)}, bf16[48,4,128]{2,1,0:T(4,128)(2,1)S(1)}, u32[]{:S(2)}, u32[]{:S(2)}) collective-permute-start(bf16[48,4,128]{2,1,0:T(4,128)(2,1)S(1)} %get-tuple-element.64), channel_id=1, source_target_pairs={{1,0},{2,1},{3,2},{0,3},{5,4},{6,5},{7,6},{4,7},{9,8},{10,9},{11,1... | collective-permute-start | bytes 147464 | tf_op jit(solution)/shard_map/ppermute | solution.py:38
  61.7 3.6 %collective-permute-start.7 = (bf16[48,4,128]{2,1,0:T(4,128)(2,1)S(1)}, bf16[48,4,128]{2,1,0:T(4,128)(2,1)S(1)}, u32[]{:S(2)}, u32[]{:S(2)}) collective-permute-start(bf16[48,4,128]{2,1,0:T(4,128)(2,1)S(1)} %get-tuple-element.59), channel_id=1, source_target_pairs={{0,1},{1,2},{2,3},{3,0},{4,5},{5,6},{6,7},{7,4},{8,9},{9,10},{10,1... | collective-permute-start | bytes 147464 | tf_op jit(solution)/shard_map/ppermute | solution.py:35
  61.7 3.5 %collective-permute-start.8 = (bf16[48,4,128]{2,1,0:T(4,128)(2,1)S(1)}, bf16[48,4,128]{2,1,0:T(4,128)(2,1)S(1)}, u32[]{:S(2)}, u32[]{:S(2)}) collective-permute-start(bf16[48,4,128]{2,1,0:T(4,128)(2,1)S(1)} %get-tuple-element.60), channel_id=1, source_target_pairs={{1,0},{2,1},{3,2},{0,3},{5,4},{6,5},{7,6},{4,7},{9,8},{10,9},{11,1... | collective-permute-start | bytes 147464 | tf_op jit(solution)/shard_map/ppermute | solution.py:38
